TPU v7x, 32 devices: a whole 2x2x4 slice. The times are simulated.
32 devices in a mesh: dp: 4 (over z), pair: 8 (over y, x, core).
Axes of the slice: x: 2, y: 2, z: 4, core: 2. Of those that a mesh axis runs over, the one named last changes fastest.
Arguments:
- embeddings: bfloat16 [128, 512, 256], P('pair', 'dp'), may hold values from -6 to 6
- field_width: int32 [128], replicated, may hold values from 64 to 256, as said below
- pair_fields: int32 [384, 2], replicated, may hold values from 0 to 127, as said below
- pair_mats: bfloat16 [384, 256, 256], P('pair'), may hold values from -0.0048828125 to 0.0048828125
- labels: int32 [512], P('dp'), may hold values 0 or 1
Outputs:
- logits: float32 [512], P('dp')
- mat_grad: bfloat16 [384, 256, 256], P('pair', 'dp')
- emb_grad: float32 [128, 512, 256], P('pair', 'dp')
Inputs may be any that keep to these rules, and one draw needn't show every extreme that they name: `field_width`: each is 64, 128 or 256. `pair_fields`: the two fields of a pair differ. The 48 pairs of one owner read at most 3 different fields from the 16 fields of any one owner (field f is owned by index f // 16), and exactly 3 from some owner.
All inputs are finite; a program needn't handle non-finite values. No bound on the sum of `labels` on one device may be relied on, other than what follows from the above.
Results may differ from a plain program's by a relative error of at most 0.017.
Values may be sent and summed in bfloat16 or wider, within the bound.
No kernel may reach another device: no remote copies, remote signals or barrier semaphores. Data moves between devices by JAX's collectives and lax.ppermute only.
A program may use at most 128 MiB of HBM per device.

v0:
```python
import jax
import jax.numpy as jnp
from jax import lax
from jax.sharding import PartitionSpec as P

CAP = 3


def shards(embeddings, field_width, pair_fields, pair_mats, labels):
    owners = lax.axis_size("pair")
    owner_index = lax.axis_index("pair")
    field_count = embeddings.shape[0]
    sample_count = embeddings.shape[1]
    padded_width = embeddings.shape[2]
    pair_count = pair_mats.shape[0]
    column_ids = jnp.arange(padded_width, dtype=jnp.int32)
    width_mask = (column_ids[None, :] < field_width[:, None]).astype(jnp.bfloat16)
    own_mask = lax.dynamic_slice_in_dim(width_mask, owner_index * field_count, field_count, 0)
    masked = embeddings * own_mask[:, None, :]
    my_fields = owner_index * field_count + jnp.arange(field_count, dtype=jnp.int32)
    grouped = pair_fields.reshape(owners, pair_count * 2)
    needed = jnp.any(grouped[:, :, None] == my_fields[None, None, :], axis=1)
    slot_rank = jnp.cumsum(needed.astype(jnp.int32), axis=1) - 1
    slot_ids = jnp.arange(CAP, dtype=jnp.int32)
    selector = (needed[:, None, :] & (slot_rank[:, None, :] == slot_ids[None, :, None])).astype(
        jnp.bfloat16
    )
    outgoing = jnp.einsum("dcf,fsk->dcsk", selector, masked, preferred_element_type=jnp.bfloat16)
    incoming = lax.all_to_all(outgoing, "pair", split_axis=0, concat_axis=0, tiled=True)
    received = incoming.reshape(owners * CAP, sample_count, padded_width)
    my_pairs = lax.dynamic_slice_in_dim(pair_fields, owner_index * pair_count, pair_count, 0)
    every_field = jnp.arange(owners * field_count, dtype=jnp.int32)
    wanted = jnp.any(my_pairs.reshape(-1)[:, None] == every_field[None, :], axis=0).reshape(
        owners, field_count
    )
    slot_table = (jnp.cumsum(wanted.astype(jnp.int32), axis=1) - 1).reshape(-1)
    slot_index = my_pairs // field_count * CAP + slot_table[my_pairs]
    left_rows = received[slot_index[:, 0]]
    right_rows = received[slot_index[:, 1]]
    projected = jnp.einsum("psk,pkl->psl", left_rows, pair_mats, preferred_element_type=jnp.float32)
    partial_value = jnp.sum(projected * right_rows, axis=(0, 2))
    logits = lax.psum(partial_value, "pair")
    grad_out = jax.nn.sigmoid(logits) - labels.astype(jnp.float32)
    toward_left = grad_out[None, :, None] * jnp.einsum(
        "psl,pkl->psk", right_rows, pair_mats, preferred_element_type=jnp.float32
    )
    toward_right = grad_out[None, :, None] * projected
    slot_grads = jnp.zeros((owners * CAP, sample_count, padded_width), jnp.float32)
    slot_grads = (
        slot_grads.at[slot_index[:, 0]].add(toward_left).at[slot_index[:, 1]].add(toward_right)
    )
    slot_grads = slot_grads.astype(jnp.bfloat16).reshape(owners, CAP, sample_count, padded_width)
    returned = lax.all_to_all(slot_grads, "pair", split_axis=0, concat_axis=0, tiled=True)
    emb_grad = jnp.einsum("dcf,dcsk->fsk", selector, returned, preferred_element_type=jnp.float32)
    emb_grad = emb_grad * own_mask[:, None, :].astype(jnp.float32)
    scaled = (grad_out[None, :, None] * left_rows).astype(jnp.bfloat16)
    mat_term = jnp.einsum("psk,psl->pkl", scaled, right_rows, preferred_element_type=jnp.float32)
    mat_grad = lax.psum_scatter(
        mat_term.astype(jnp.bfloat16), "dp", scatter_dimension=1, tiled=True
    )
    return (logits, mat_grad, emb_grad)


def solution(mesh):
    in_specs = (P("pair", "dp", None), P(), P(), P("pair", None, None), P("dp"))
    out_specs = (P("dp"), P("pair", "dp", None), P("pair", "dp", None))
    return jax.shard_map(shards, mesh=mesh, in_specs=in_specs, out_specs=out_specs, check_vma=False)
```

profile of v0, /device:TPU:0, one launch (start us, length us, event | category | flops | bytes accessed | tf_op | source)
XLA Modules:
  0.0 190.4 jit_solution(742963178127088369)
XLA Ops:
  7.2 0.7 dynamic-slice
  8.0 0.8 copy.34
  8.8 0.1 eq.43
  9.0 0.3 compare_reduce_fusion
  9.2 0.2 reduce_window_sum.17
  9.4 1.3 broadcast_multiply_fusion.2
  10.7 0.7 fusion.2
  11.5 1.5 copy.36
  13.0 5.2 %all-to-all-start = ((bf16[8,3,128,256]{3,2,1,0:T(8,128)(2,1)}), bf16[8,3,128,256]{3,2,1,0:T(8,128)(2,1)S(1)}, u32[]{:S(2)}, u32[]{:S(2)}) async-start(bf16[8,3,128,256]{3,2,1,0:T(8,128)(2,1)} %copy.36), calls=%async_computation | async-start | bytes 3145728 | tf_op jit(solution)/shard_map/all_to_all | solution.py:29
  18.2 0.1 eq.50
  18.5 0.2 reduce_window_sum.18
  18.8 0.1 reshape.45
  18.9 1.2 gather_fusion
  20.2 0.1 reshape.44
  20.3 0.2 fusion.10
  20.5 18.7 %all-to-all-done = bf16[8,3,128,256]{3,2,1,0:T(8,128)(2,1)S(1)} async-done(((bf16[8,3,128,256]{3,2,1,0:T(8,128)(2,1)}), bf16[8,3,128,256]{3,2,1,0:T(8,128)(2,1)S(1)}, u32[]{:S(2)}, u32[]{:S(2)}) %all-to-all-start) | async-done | bytes 1572896 | tf_op jit(solution)/shard_map/all_to_all | solution.py:29
  39.2 1.1 copy-done
  40.3 2.2 %gather_fusion.2 = bf16[48,128,256]{2,1,0:T(8,128)(2,1)S(1)} fusion(bf16[24,128,256]{2,1,0:T(8,128)(2,1)} %bitcast.20, s32[1024]{0:T(1024)S(1)} %get-tuple-element.26), kind=kCustom, calls=%fused_computation.2 | custom fusion | bytes 6291648 | tf_op jit(solution)/shard_map/gather | solution.py:39
  42.5 3.9 %gather_fusion.1 = bf16[48,128,256]{2,1,0:T(8,128)(2,1)} fusion(bf16[24,128,256]{2,1,0:T(8,128)(2,1)} %bitcast.21, s32[1024]{0:T(1024)S(1)} %get-tuple-element.27), kind=kCustom, calls=%fused_computation.1 | custom fusion | bytes 6291648 | tf_op jit(solution)/shard_map/gather | solution.py:38
  46.4 7.4 %multiply_reduce_fusion = (f32[128]{0:T(128)S(1)}, f32[48,128,256]{2,1,0:T(8,128)}) fusion(bf16[48,128,256]{2,1,0:T(8,128)(2,1)S(1)} %gather_fusion.2, bf16[48,128,256]{2,1,0:T(8,128)(2,1)} %gather_fusion.1, bf16[48,256,256]{2,1,0:T(8,128)(2,1)} %param.8), kind=kOutput, calls=%fused_computation.6 | convolution fusion | flops 810024832 | bytes 18874880 | tf_op jit(solution)/shard_map/psk,pkl->psl/dot_general | solution.py:40
  53.8 11.8 %psum.7 = f32[128]{0:T(128)S(1)} all-reduce(f32[128]{0:T(128)S(1)} %get-tuple-element.24), channel_id=1, replica_groups=mesh['dp'=4,'pair'=8] {'pair'}, use_global_device_ids=true, to_apply=%region_5.6 | all-reduce | flops 128 | bytes 1024 | tf_op jit(solution)/shard_map/psum | solution.py:42
  65.6 6.5 %convolution_convert_fusion = bf16[48,256,256]{2,1,0:T(8,128)(2,1)} fusion(bf16[48,128,256]{2,1,0:T(8,128)(2,1)S(1)} %gather_fusion.2, bf16[48,128,256]{2,1,0:T(8,128)(2,1)} %gather_fusion.1, f32[128]{0:T(128)S(1)} %divide_subtract_fusion), kind=kOutput, calls=%fused_computation.7 | convolution fusion | flops 813170688 | bytes 12583424 | tf_op jit(solution)/shard_map/psk,psl->pkl/dot_general | solution.py:57
  72.2 8.2 %broadcast_multiply_fusion.1 = f32[48,128,256]{2,1,0:T(8,128)} fusion(f32[128]{0:T(128)S(1)} %divide_subtract_fusion, bf16[48,128,256]{2,1,0:T(8,128)(2,1)S(1)} %gather_fusion.2, bf16[48,256,256]{2,1,0:T(8,128)(2,1)} %param.8), kind=kOutput, calls=%fused_computation.9 | convolution fusion | flops 806879232 | bytes 15729152 | tf_op jit(solution)/shard_map/psl,pkl->psk/dot_general | solution.py:44
  80.4 0.3 broadcast_in_dim.5
  80.8 9.5 %scatter_fusion = f32[24,128,256]{2,1,0:T(8,128)S(1)} fusion(f32[24,128,256]{2,1,0:T(8,128)S(1)} %broadcast_in_dim.5, s32[48]{0:T(128)S(1)} %get-tuple-element.19, f32[48,128,256]{2,1,0:T(8,128)} %broadcast_multiply_fusion.1), kind=kCustom, calls=%fused_computation.3 | custom fusion | flops 1572864 | bytes 18874560 | tf_op jit(solution)/shard_map/scatter-add | solution.py:50
  90.3 6.5 %broadcast_multiply_fusion = f32[48,128,256]{2,1,0:T(8,128)} fusion(f32[48,128,256]{2,1,0:T(8,128)} %get-tuple-element.25, f32[128]{0:T(128)S(1)} %divide_subtract_fusion), kind=kLoop, calls=%fused_computation.8 | loop fusion | flops 1572864 | bytes 12583424 | tf_op jit(solution)/shard_map/mul | solution.py:47
  96.8 9.5 %scatter_fusion.1 = f32[24,128,256]{2,1,0:T(8,128)S(1)} fusion(f32[24,128,256]{2,1,0:T(8,128)S(1)} %scatter_fusion, s32[48]{0:T(128)S(1)} %get-tuple-element.18, f32[48,128,256]{2,1,0:T(8,128)} %broadcast_multiply_fusion), kind=kCustom, calls=%fused_computation.4 | custom fusion | flops 1572864 | bytes 18874560 | tf_op jit(solution)/shard_map/scatter-add | solution.py:50
  106.2 0.2 convert_element_type.48
  106.5 23.7 %all_to_all.10 = bf16[8,3,128,256]{3,2,1,0:T(8,128)(2,1)S(1)} all-to-all(bf16[8,3,128,256]{3,2,1,0:T(8,128)(2,1)S(1)} %bitcast.22), channel_id=1, replica_groups=mesh['dp'=4,'pair'=8] {'pair'}, dimensions={0} | all-to-all | bytes 3145728 | tf_op jit(solution)/shard_map/all_to_all | solution.py:53
  130.1 1.0 bitcast_multiply_fusion
  131.1 2.5 %copy.40 = f32[16,128,256]{2,1,0:T(8,128)} copy(f32[16,128,256]{2,0,1:T(8,128)S(1)} %bitcast_multiply_fusion) | data formatting | bytes 4194304
  133.7 49.9 %reduce-scatter.2.cloned.1.call-done = bf16[48,64,256]{2,1,0:T(8,128)(2,1)} async-done(((bf16[48,256,256]{2,1,0:T(8,128)(2,1)}), bf16[48,64,256]{2,1,0:T(8,128)(2,1)}) %reduce-scatter.2.cloned.1.call-update) | async-done | bytes 1572880 | tf_op jit(solution)/shard_map/reduce_scatter | solution.py:58
  (21 shorter events, 0.5 us)
Async XLA Ops:
  13.0 26.2 %all-to-all-start = ((bf16[8,3,128,256]{3,2,1,0:T(8,128)(2,1)}), bf16[8,3,128,256]{3,2,1,0:T(8,128)(2,1)S(1)}, u32[]{:S(2)}, u32[]{:S(2)}) async-start(bf16[8,3,128,256]{3,2,1,0:T(8,128)(2,1)} %copy.36), calls=%async_computation | async-start | bytes 3145728 | tf_op jit(solution)/shard_map/all_to_all | solution.py:29
  18.2 165.4 %reduce-scatter.2.cloned.1.call-start = ((), (), s32[]{:S(2)}) async-start(), calls=%async_computation.3 | async-start | bytes 7864320 | tf_op jit(solution)/shard_map/reduce_scatter | solution.py:58
  39.2 1.1 copy-start
  46.4 19.2 %copy-start.1 = (s32[128]{0:T(128)S(1)}, s32[128]{0:T(128)}, u32[]{:S(2)}) copy-start(s32[128]{0:T(128)} %param.9) | copy-start | bytes 1540
  65.6 6.6 %copy-start.2 = (f32[128]{0:T(128)}, f32[128]{0:T(128)S(1)}, u32[]{:S(2)}) copy-start(f32[128]{0:T(128)S(1)} %psum.7) | copy-start | bytes 1540
Sparse Core Ops, SparseCore 0:
  72.3 111.1 reduce-scatter.1
where the time goes:
time: 191 us; the launch traced here: 190 us
  waiting for transfers between devices  68.6 us (36%)
  blocking collectives  35.4 us (19%)
  other arithmetic  28 us (15%)
  matrix products  23.9 us (13%)
  local copies, waits for them, and re-layouts  15 us (8%)
  between operations  14.2 us (7%)
  starting transfers between devices  5.21 us (3%)
    reduce_scatter x1, waiting for transfers between devices, shards(): lax.psum_scatter(mat_term.astype(jnp.bfloat16), 'dp', scatter_dimension=1...  49.9 us
    all_to_all x1, blocking collectives, shards(): lax.all_to_all(slot_grads, 'pair', split_axis=0, concat_axis=0, tiled=True)  23.7 us
    scatter-add x2, other arithmetic, shards(): slot_grads.at[slot_index[:, 0]].add(toward_left).at[slot_index[:, 1]]  19 us
    all_to_all x1, waiting for transfers between devices, shards(): lax.all_to_all(outgoing, 'pair', split_axis=0, concat_axis=0, tiled=True)  18.7 us
    psum x1, blocking collectives, shards(): logits = lax.psum(partial_value, 'pair')  11.8 us
    dot_general x1, matrix products, shards(): jnp.einsum('psl,pkl->psk', right_rows, pair_mats, preferred_element_type=...  8.23 us
    dot_general x1, matrix products, shards(): jnp.einsum('psk,pkl->psl', left_rows, pair_mats, preferred_element_type=j...  7.41 us
    dot_general x1, matrix products, shards(): jnp.einsum('psk,psl->pkl', scaled, right_rows, preferred_element_type=jnp...  6.53 us
  transfers between devices with their start and end apart: 2, of which 2 were waited for; matrix products, arithmetic and copies ran while one was open for 21% of the time, Pallas kernels for 0%

commit v1 on v0

--- a/solution.py
+++ b/solution.py
@@ -4,6 +4,15 @@
 from jax.sharding import PartitionSpec as P
 
 CAP = 3
+
+
+def add_in_pairs(value, name):
+    devices = lax.axis_size(name)
+    result, far = (value, 1)
+    while far < devices:
+        result = result + lax.ppermute(result, name, [(i, i ^ far) for i in range(devices)])
+        far = 2 * far
+    return result
 
 
 def shards(embeddings, field_width, pair_fields, pair_mats, labels):
@@ -39,7 +48,7 @@
     right_rows = received[slot_index[:, 1]]
     projected = jnp.einsum("psk,pkl->psl", left_rows, pair_mats, preferred_element_type=jnp.float32)
     partial_value = jnp.sum(projected * right_rows, axis=(0, 2))
-    logits = lax.psum(partial_value, "pair")
+    logits = add_in_pairs(partial_value, "pair")
     grad_out = jax.nn.sigmoid(logits) - labels.astype(jnp.float32)
     toward_left = grad_out[None, :, None] * jnp.einsum(
         "psl,pkl->psk", right_rows, pair_mats, preferred_element_type=jnp.float32

time: 191 us -> 185 us (0.969)
  blocking collectives: 35.4 us -> 23.4 us
  waiting for transfers between devices: 68.6 us -> 75.2 us
    psum x1 -> x0, blocking collectives: 11.8 us -> none  [shards(): logits = lax.psum(partial_value, 'pair')]
    ppermute x0 -> x3, waiting for transfers between devices: none -> 7.13 us  [add_in_pairs(): lax.ppermute(result, name, [(i, i ^ far) for i in range(devices)])]
  transfers between devices with their start and end apart: 2 -> 5, of which waited for: 2 -> 5; matrix products, arithmetic and copies ran while one was open for 21% -> 21% of each run, Pallas kernels for 0% -> 0%
where the time goes in v1:
time: 185 us
  waiting for transfers between devices  75.2 us (41%)
  other arithmetic  28.5 us (15%)
  blocking collectives  23.4 us (13%)
  matrix products  22 us (12%)
  local copies, waits for them, and re-layouts  15.1 us (8%)
  between operations  14.2 us (8%)
  starting transfers between devices  6.28 us (3%)
    reduce_scatter x1, waiting for transfers between devices, shards(): lax.psum_scatter(mat_term.astype(jnp.bfloat16), 'dp', scatter_dimension=1...  49.4 us
    all_to_all x1, blocking collectives, shards(): lax.all_to_all(slot_grads, 'pair', split_axis=0, concat_axis=0, tiled=True)  23.4 us
    scatter-add x2, other arithmetic, shards(): slot_grads.at[slot_index[:, 0]].add(toward_left).at[slot_index[:, 1]]  19 us
    all_to_all x1, waiting for transfers between devices, shards(): lax.all_to_all(outgoing, 'pair', split_axis=0, concat_axis=0, tiled=True)  18.7 us
    dot_general x1, matrix products, shards(): jnp.einsum('psl,pkl->psk', right_rows, pair_mats, preferred_element_type=...  7.97 us
    dot_general x1, matrix products, shards(): jnp.einsum('psk,pkl->psl', left_rows, pair_mats, preferred_element_type=j...  7.54 us
    ppermute x3, waiting for transfers between devices, add_in_pairs(): lax.ppermute(result, name, [(i, i ^ far) for i in range(devices)])  7.13 us
    mul x1, other arithmetic, shards(): toward_right = grad_out[None, :, None] * projected  6.36 us
  transfers between devices with their start and end apart: 5, of which 5 were waited for; matrix products, arithmetic and copies ran while one was open for 21% of the time, Pallas kernels for 0%

profile of v1, /device:TPU:0, one launch (start us, length us, event | category | flops | bytes accessed | tf_op | source)
XLA Modules:
  0.0 184.7 jit_solution(2902397970083209178)
XLA Ops:
  7.2 0.7 dynamic-slice
  8.0 0.8 copy.34
  9.0 0.3 compare_reduce_fusion
  9.4 1.3 broadcast_multiply_fusion.2
  10.7 0.7 fusion.2
  11.5 1.5 copy.36
  13.0 5.2 %all-to-all-start = ((bf16[8,3,128,256]{3,2,1,0:T(8,128)(2,1)}), bf16[8,3,128,256]{3,2,1,0:T(8,128)(2,1)S(1)}, u32[]{:S(2)}, u32[]{:S(2)}) async-start(bf16[8,3,128,256]{3,2,1,0:T(8,128)(2,1)} %copy.36), calls=%async_computation | async-start | bytes 3145728 | tf_op jit(solution)/shard_map/all_to_all | solution.py:38
  18.5 0.2 reduce_window_sum.18
  18.9 1.2 gather_fusion
  20.3 0.2 fusion.10
  20.5 18.7 %all-to-all-done = bf16[8,3,128,256]{3,2,1,0:T(8,128)(2,1)S(1)} async-done(((bf16[8,3,128,256]{3,2,1,0:T(8,128)(2,1)}), bf16[8,3,128,256]{3,2,1,0:T(8,128)(2,1)S(1)}, u32[]{:S(2)}, u32[]{:S(2)}) %all-to-all-start) | async-done | bytes 1572896 | tf_op jit(solution)/shard_map/all_to_all | solution.py:38
  39.2 1.1 copy-done
  40.3 2.2 %gather_fusion.2 = bf16[48,128,256]{2,1,0:T(8,128)(2,1)S(1)} fusion(bf16[24,128,256]{2,1,0:T(8,128)(2,1)} %bitcast.20, s32[1024]{0:T(1024)S(1)} %get-tuple-element.28), kind=kCustom, calls=%fused_computation.2 | custom fusion | bytes 6291648 | tf_op jit(solution)/shard_map/gather | solution.py:48
  42.5 4.0 %gather_fusion.1 = bf16[48,128,256]{2,1,0:T(8,128)(2,1)} fusion(bf16[24,128,256]{2,1,0:T(8,128)(2,1)} %bitcast.21, s32[1024]{0:T(1024)S(1)} %get-tuple-element.29), kind=kCustom, calls=%fused_computation.1 | custom fusion | bytes 6291648 | tf_op jit(solution)/shard_map/gather | solution.py:47
  46.5 7.5 %multiply_reduce_fusion = (f32[128]{0:T(128)S(1)}, f32[48,128,256]{2,1,0:T(8,128)}) fusion(bf16[48,128,256]{2,1,0:T(8,128)(2,1)S(1)} %gather_fusion.2, bf16[48,128,256]{2,1,0:T(8,128)(2,1)} %gather_fusion.1, bf16[48,256,256]{2,1,0:T(8,128)(2,1)} %param.8), kind=kOutput, calls=%fused_computation.6 | convolution fusion | flops 810024832 | bytes 18874880 | tf_op jit(solution)/shard_map/psk,pkl->psl/dot_general | solution.py:49
  54.0 1.1 collective-permute-done
  55.1 0.5 collective-permute-start.1
  55.6 3.0 %collective-permute-done.1 = f32[128]{0:T(128)S(1)} collective-permute-done((f32[128]{0:T(128)S(1)}, f32[128]{0:T(128)S(1)}, u32[]{:S(2)}, u32[]{:S(2)}) %collective-permute-start.1) | collective-permute-done | bytes 544 | tf_op jit(solution)/shard_map/ppermute | solution.py:13
  58.7 0.6 collective-permute-start.2
  59.2 3.0 %collective-permute-done.2 = f32[128]{0:T(128)S(1)} collective-permute-done((f32[128]{0:T(128)S(1)}, f32[128]{0:T(128)S(1)}, u32[]{:S(2)}, u32[]{:S(2)}) %collective-permute-start.2) | collective-permute-done | bytes 544 | tf_op jit(solution)/shard_map/ppermute | solution.py:13
  62.2 0.5 divide_subtract_fusion
  62.7 4.8 %convolution_convert_fusion = bf16[48,256,256]{2,1,0:T(8,128)(2,1)} fusion(bf16[48,128,256]{2,1,0:T(8,128)(2,1)S(1)} %gather_fusion.2, bf16[48,128,256]{2,1,0:T(8,128)(2,1)S(1)} %copy-done.1, f32[128]{0:T(128)S(1)} %get-tuple-element.20), kind=kOutput, calls=%fused_computation.7 | convolution fusion | flops 813170688 | bytes 12583424 | tf_op jit(solution)/shard_map/psk,psl->pkl/dot_general | solution.py:66
  67.5 8.0 %broadcast_multiply_fusion.1 = f32[48,128,256]{2,1,0:T(8,128)} fusion(f32[128]{0:T(128)S(1)} %get-tuple-element.20, bf16[48,128,256]{2,1,0:T(8,128)(2,1)S(1)} %gather_fusion.2, bf16[48,256,256]{2,1,0:T(8,128)(2,1)} %param.8), kind=kOutput, calls=%fused_computation.9 | convolution fusion | flops 806879232 | bytes 15729152 | tf_op jit(solution)/shard_map/psl,pkl->psk/dot_general | solution.py:53
  75.5 0.3 broadcast_in_dim.5
  75.8 9.5 %scatter_fusion = f32[24,128,256]{2,1,0:T(8,128)S(1)} fusion(f32[24,128,256]{2,1,0:T(8,128)S(1)} %broadcast_in_dim.5, s32[48]{0:T(128)S(1)} %get-tuple-element.19, f32[48,128,256]{2,1,0:T(8,128)} %broadcast_multiply_fusion.1), kind=kCustom, calls=%fused_computation.3 | custom fusion | flops 1572864 | bytes 18874560 | tf_op jit(solution)/shard_map/scatter-add | solution.py:59
  85.4 6.4 %broadcast_multiply_fusion = f32[48,128,256]{2,1,0:T(8,128)} fusion(f32[48,128,256]{2,1,0:T(8,128)} %get-tuple-element.27, f32[128]{0:T(128)S(1)} %get-tuple-element.20), kind=kLoop, calls=%fused_computation.8 | loop fusion | flops 1572864 | bytes 12583424 | tf_op jit(solution)/shard_map/mul | solution.py:56
  91.8 9.5 %scatter_fusion.1 = f32[24,128,256]{2,1,0:T(8,128)S(1)} fusion(f32[24,128,256]{2,1,0:T(8,128)S(1)} %scatter_fusion, s32[48]{0:T(128)S(1)} %get-tuple-element.18, f32[48,128,256]{2,1,0:T(8,128)} %broadcast_multiply_fusion), kind=kCustom, calls=%fused_computation.4 | custom fusion | flops 1572864 | bytes 18874560 | tf_op jit(solution)/shard_map/scatter-add | solution.py:59
  101.2 0.2 convert_element_type.48
  101.5 23.4 %all_to_all.10 = bf16[8,3,128,256]{3,2,1,0:T(8,128)(2,1)S(1)} all-to-all(bf16[8,3,128,256]{3,2,1,0:T(8,128)(2,1)S(1)} %bitcast.22), channel_id=1, replica_groups=mesh['dp'=4,'pair'=8] {'pair'}, dimensions={0} | all-to-all | bytes 3145728 | tf_op jit(solution)/shard_map/all_to_all | solution.py:62
  124.9 1.0 bitcast_multiply_fusion
  125.9 2.5 %copy.40 = f32[16,128,256]{2,1,0:T(8,128)} copy(f32[16,128,256]{2,0,1:T(8,128)S(1)} %bitcast_multiply_fusion) | data formatting | bytes 4194304
  128.4 49.4 %reduce-scatter.2.cloned.1.call-done = bf16[48,64,256]{2,1,0:T(8,128)(2,1)} async-done(((bf16[48,256,256]{2,1,0:T(8,128)(2,1)}), bf16[48,64,256]{2,1,0:T(8,128)(2,1)}) %reduce-scatter.2.cloned.1.call-update) | async-done | bytes 1572880 | tf_op jit(solution)/shard_map/reduce_scatter | solution.py:67
  (28 shorter events, 1.1 us)
Async XLA Ops:
  13.0 26.2 %all-to-all-start = ((bf16[8,3,128,256]{3,2,1,0:T(8,128)(2,1)}), bf16[8,3,128,256]{3,2,1,0:T(8,128)(2,1)S(1)}, u32[]{:S(2)}, u32[]{:S(2)}) async-start(bf16[8,3,128,256]{3,2,1,0:T(8,128)(2,1)} %copy.36), calls=%async_computation | async-start | bytes 3145728 | tf_op jit(solution)/shard_map/all_to_all | solution.py:38
  18.2 159.7 %reduce-scatter.2.cloned.1.call-start = ((), (), s32[]{:S(2)}) async-start(), calls=%async_computation.3 | async-start | bytes 7864320 | tf_op jit(solution)/shard_map/reduce_scatter | solution.py:67
  39.2 1.1 copy-start
  46.4 15.8 %copy-start.2 = (s32[128]{0:T(128)S(1)}, s32[128]{0:T(128)}, u32[]{:S(2)}) copy-start(s32[128]{0:T(128)} %param.9) | copy-start | bytes 1540
  46.4 16.3 %copy-start.1 = (bf16[48,128,256]{2,1,0:T(8,128)(2,1)S(1)}, bf16[48,128,256]{2,1,0:T(8,128)(2,1)}, u32[]{:S(2)}) copy-start(bf16[48,128,256]{2,1,0:T(8,128)(2,1)} %gather_fusion.1) | copy-start | bytes 9437188
  54.0 1.1 collective-permute-start
  55.1 3.5 %collective-permute-start.1 = (f32[128]{0:T(128)S(1)}, f32[128]{0:T(128)S(1)}, u32[]{:S(2)}, u32[]{:S(2)}) collective-permute-start(f32[128]{0:T(128)S(1)} %add.71), channel_id=1, source_target_pairs={{0,2},{1,3},{2,0},{3,1},{4,6},{5,7},{6,4},{7,5},{8,10},{9,11},{10,... | collective-permute-start | bytes 1544 | tf_op jit(solution)/shard_map/ppermute | solution.py:13
  58.7 3.5 %collective-permute-start.2 = (f32[128]{0:T(128)S(1)}, f32[128]{0:T(128)S(1)}, u32[]{:S(2)}, u32[]{:S(2)}) collective-permute-start(f32[128]{0:T(128)S(1)} %add.72), channel_id=1, source_target_pairs={{0,4},{1,5},{2,6},{3,7},{4,0},{5,1},{6,2},{7,3},{8,12},{9,13},{10,... | collective-permute-start | bytes 1544 | tf_op jit(solution)/shard_map/ppermute | solution.py:13
Sparse Core Ops, SparseCore 0:
  67.7 110.1 reduce-scatter.1
